TPU v7x, 32 devices: a whole 2x2x4 slice. The times are simulated.
32 devices in a mesh: row: 8 (over z, y), col: 4 (over x, core).
Axes of the slice: x: 2, y: 2, z: 4, core: 2. Of those that a mesh axis runs over, the one named last changes fastest.
Arguments:
- weights: bfloat16 [24576, 24576], P('row', 'col'), may hold values from -0.0390625 to 0.0390625
- rates: bfloat16 [5, 24576, 128], P(None, 'col'), may hold values from -0.94921875 to 0.94921875
Outputs:
- weight_grad: bfloat16 [24576, 24576], P('row', 'col')
All inputs are finite; a program needn't handle non-finite values.
Results may differ from a plain program's by a relative error of at most 0.02.
Values may be sent and summed in bfloat16 or wider, within the bound.
A program may use at most 384 MiB of HBM per device.

v0:
```python
import jax
import jax.numpy as jnp
from jax import lax
from jax.sharding import PartitionSpec as P

STEPS = 4


def spread(block, axis, owner):
    block = jnp.where(lax.axis_index(axis) == owner, block, jnp.zeros_like(block))
    return lax.psum(block, axis)


def per_device(weights, rates):
    row_block = weights.shape[0]
    col_block = weights.shape[1]
    per_col = col_block // row_block
    row_index = lax.axis_index("row")
    root_col = row_index // per_col
    offset = row_index % per_col * row_block
    ratef = rates.astype(jnp.float32)
    forcing = ratef[STEPS] - ratef[0]
    own_rates = lax.dynamic_slice_in_dim(ratef[STEPS], offset, row_block, 0)
    forcing_rows = lax.dynamic_slice_in_dim(forcing, offset, row_block, 0)
    grad_slice = (forcing_rows * (1.0 - own_rates * own_rates)).astype(jnp.bfloat16)
    accum = jnp.zeros((row_block, col_block), jnp.float32)
    for step in range(STEPS, 0, -1):
        grad_here = spread(grad_slice, "col", root_col)
        accum = accum + lax.dot_general(
            grad_here, rates[step - 1], (((1,), (1,)), ((), ())), preferred_element_type=jnp.float32
        )
        if step > 1:
            partial_sum = lax.dot_general(
                weights, grad_here, (((0,), (0,)), ((), ())), preferred_element_type=jnp.float32
            )
            earlier = ratef[step - 1]
            adjoint = lax.psum(partial_sum.astype(jnp.bfloat16), "row").astype(jnp.float32)
            adjoint_rows = lax.dynamic_slice_in_dim(adjoint, offset, row_block, 0)
            earlier_rows = lax.dynamic_slice_in_dim(earlier, offset, row_block, 0)
            grad_slice = (adjoint_rows * (1.0 - earlier_rows * earlier_rows)).astype(jnp.bfloat16)
    return accum.astype(jnp.bfloat16)


def solution(mesh):
    in_specs = (P("row", "col"), P(None, "col", None))
    out_specs = P("row", "col")
    return jax.shard_map(
        per_device, mesh=mesh, in_specs=in_specs, out_specs=out_specs, check_vma=False
    )
```

profile of v0, /device:TPU:7, one launch (start us, length us, event | category | flops | bytes accessed | tf_op | source)
XLA Modules:
  0.0 577.6 jit_solution(5603566821357512998)
XLA Ops:
  6.5 10.6 %copy.3 = bf16[5,6144,128]{1,2,0:T(8,128)(2,1)} copy(bf16[5,6144,128]{2,1,0:T(8,128)(2,1)} %param.3) | data formatting | bytes 15728640 | tf_op args[1]
  17.1 8.9 %fusion.24 = (f32[1,6144,128]{1,2,0:T(8,128)S(1)}, f32[1,6144,128]{1,2,0:T(8,128)}, f32[1,6144,128]{1,2,0:T(8,128)}, f32[1,6144,128]{1,2,0:T(8,128)}, f32[1,6144,128]{1,2,0:T(8,128)}) fusion(bf16[5,6144,128]{1,2,0:T(8,128)(2,1)} %copy.3), kind=kLoop, calls=%fused_computation.32 | loop fusion | bytes 31457280 | tf_op jit(solution)/shard_map/slice | solution.py:36
  26.0 3.1 fusion.23
  29.1 0.0 all-reduce.8.cloned.1.call-update
  29.1 0.0 all-reduce.10.cloned.1.call-start
  29.1 34.6 %all-reduce.8.cloned.1.call-done = bf16[3072,128]{0,1:T(8,128)(2,1)} async-done(((bf16[3072,128]{0,1:T(8,128)(2,1)}), bf16[3072,128]{0,1:T(8,128)(2,1)}) %all-reduce.8.cloned.1.call-update) | async-done | bytes 786448 | tf_op jit(solution)/shard_map/psum | solution.py:11
  63.8 15.7 %fusion = bf16[6144,128]{0,1:T(8,128)(2,1)} fusion(bf16[3072,128]{0,1:T(8,128)(2,1)} %all-reduce.8.cloned.1.call-done, bf16[3072,6144]{1,0:T(8,128)(2,1)} %param.2), kind=kOutput, calls=%fused_computation.4 | convolution fusion | flops 4832624640 | bytes 40108032 | tf_op jit(solution)/shard_map/dot_general | solution.py:33
  79.5 0.0 all-reduce.12.cloned.1.call-start
  79.6 90.5 %all-reduce.10.cloned.1.call-done = bf16[6144,128]{0,1:T(8,128)(2,1)} async-done(((bf16[6144,128]{0,1:T(8,128)(2,1)}), bf16[6144,128]{0,1:T(8,128)(2,1)}) %all-reduce.10.cloned.1.call-update) | async-done | bytes 1572880 | tf_op jit(solution)/shard_map/psum | solution.py:37
  170.1 2.8 fusion.19
  172.9 0.0 all-reduce.12.cloned.1.call-update
  172.9 0.0 all-reduce.14.cloned.1.call-start
  172.9 32.6 %all-reduce.12.cloned.1.call-done = bf16[3072,128]{0,1:T(8,128)(2,1)} async-done(((bf16[3072,128]{0,1:T(8,128)(2,1)}), bf16[3072,128]{0,1:T(8,128)(2,1)}) %all-reduce.12.cloned.1.call-update) | async-done | bytes 786448 | tf_op jit(solution)/shard_map/psum | solution.py:11
  205.5 15.7 %fusion.1 = bf16[6144,128]{0,1:T(8,128)(2,1)} fusion(bf16[3072,128]{0,1:T(8,128)(2,1)} %all-reduce.12.cloned.1.call-done, bf16[3072,6144]{1,0:T(8,128)(2,1)} %param.2), kind=kOutput, calls=%fused_computation.5 | convolution fusion | flops 4832624640 | bytes 40108032 | tf_op jit(solution)/shard_map/dot_general | solution.py:33
  221.3 0.0 all-reduce.14.cloned.1.call-update
  221.3 0.0 all-reduce.16.cloned.1.call-start
  221.3 90.5 %all-reduce.14.cloned.1.call-done = bf16[6144,128]{0,1:T(8,128)(2,1)} async-done(((bf16[6144,128]{0,1:T(8,128)(2,1)}), bf16[6144,128]{0,1:T(8,128)(2,1)}) %all-reduce.14.cloned.1.call-update) | async-done | bytes 1572880 | tf_op jit(solution)/shard_map/psum | solution.py:37
  311.9 2.8 fusion.20
  314.6 0.0 all-reduce.16.cloned.1.call-update
  314.7 0.2 all-reduce.18.cloned.1.call-start
  314.9 29.0 %fusion.13 = f32[3072,6144]{1,0:T(8,128)} fusion(bf16[3072,128]{0,1:T(8,128)(2,1)} %all-reduce.8.cloned.1.call-done, bf16[5,6144,128]{2,1,0:T(8,128)(2,1)} %param.3), kind=kOutput, calls=%fused_computation.21 | convolution fusion | flops 4831838208 | bytes 77856768 | tf_op jit(solution)/shard_map/dot_general | solution.py:29
  343.9 3.4 all-reduce.16.cloned.1.call-done
  347.3 15.7 %fusion.2 = bf16[6144,128]{0,1:T(8,128)(2,1)} fusion(bf16[3072,128]{0,1:T(8,128)(2,1)} %all-reduce.16.cloned.1.call-done, bf16[3072,6144]{1,0:T(8,128)(2,1)} %param.2), kind=kOutput, calls=%fused_computation.6 | convolution fusion | flops 4832624640 | bytes 40108032 | tf_op jit(solution)/shard_map/dot_general | solution.py:33
  363.0 0.0 all-reduce.18.cloned.1.call-update
  363.1 0.3 all-reduce.20.cloned.1.call-start
  363.3 29.2 %fusion.10 = f32[3072,6144]{1,0:T(8,128)} fusion(bf16[3072,128]{0,1:T(8,128)(2,1)} %all-reduce.12.cloned.1.call-done, bf16[5,6144,128]{2,1,0:T(8,128)(2,1)} %param.3), kind=kOutput, calls=%fused_computation.17 | convolution fusion | flops 4831838208 | bytes 77856768 | tf_op jit(solution)/shard_map/dot_general | solution.py:29
  392.5 61.1 %all-reduce.18.cloned.1.call-done = bf16[6144,128]{0,1:T(8,128)(2,1)} async-done(((bf16[6144,128]{0,1:T(8,128)(2,1)}), bf16[6144,128]{0,1:T(8,128)(2,1)}) %all-reduce.18.cloned.1.call-update) | async-done | bytes 1572880 | tf_op jit(solution)/shard_map/psum | solution.py:37
  453.7 2.3 fusion.21
  456.0 0.0 all-reduce.20.cloned.1.call-update
  456.0 29.0 %fusion.7 = f32[3072,6144]{1,0:T(8,128)} fusion(bf16[3072,128]{0,1:T(8,128)(2,1)} %all-reduce.16.cloned.1.call-done, bf16[5,6144,128]{2,1,0:T(8,128)(2,1)} %param.3), kind=kOutput, calls=%fused_computation.13 | convolution fusion | flops 4831838208 | bytes 77856768 | tf_op jit(solution)/shard_map/dot_general | solution.py:29
  485.1 3.6 all-reduce.20.cloned.1.call-done
  488.6 82.1 %add_convert_fusion = bf16[3072,6144]{1,0:T(8,128)(2,1)} fusion(f32[3072,6144]{1,0:T(8,128)} %fusion.7, f32[3072,6144]{1,0:T(8,128)} %fusion.13, f32[3072,6144]{1,0:T(8,128)} %fusion.10, bf16[3072,128]{0,1:T(8,128)(2,1)} %all-reduce.20.cloned.1.call-done, bf16[5,6144,128]{2,1,0:T(8,128)(2,1)} %param.3), kind=kOutput, calls=%fused_computation | convolution fusion | flops 4907335680 | bytes 266600448 | tf_op jit(solution)/shard_map/dot_general | solution.py:29
  (2 shorter events, 0.0 us)
Async XLA Ops:
  6.5 57.2 %all-reduce.8.cloned.1.call-start = ((), (), s32[]{:S(2)}) async-start(), calls=%async_computation | async-start | bytes 1572864 | tf_op jit(solution)/shard_map/psum | solution.py:11
  29.1 141.0 %all-reduce.10.cloned.1.call-start = ((), (), s32[]{:S(2)}) async-start(), calls=%async_computation.1 | async-start | bytes 3145728 | tf_op jit(solution)/shard_map/psum | solution.py:37
  79.5 126.0 %all-reduce.12.cloned.1.call-start = ((), (), s32[]{:S(2)}) async-start(), calls=%async_computation.2 | async-start | bytes 1572864 | tf_op jit(solution)/shard_map/psum | solution.py:11
  172.9 139.0 %all-reduce.14.cloned.1.call-start = ((), (), s32[]{:S(2)}) async-start(), calls=%async_computation.3 | async-start | bytes 3145728 | tf_op jit(solution)/shard_map/psum | solution.py:37
  221.3 126.0 %all-reduce.16.cloned.1.call-start = ((), (), s32[]{:S(2)}) async-start(), calls=%async_computation.4 | async-start | bytes 1572864 | tf_op jit(solution)/shard_map/psum | solution.py:11
  314.7 139.0 %all-reduce.18.cloned.1.call-start = ((), (), s32[]{:S(2)}) async-start(), calls=%async_computation.5 | async-start | bytes 3145728 | tf_op jit(solution)/shard_map/psum | solution.py:37
  363.1 125.6 %all-reduce.20.cloned.1.call-start = ((), (), s32[]{:S(2)}) async-start(), calls=%async_computation.6 | async-start | bytes 1572864 | tf_op jit(solution)/shard_map/psum | solution.py:11
Sparse Core Ops, SparseCore 0:
  29.2 34.4 all-reduce.7
  79.6 90.4 all-reduce.9
  173.0 32.4 all-reduce.11
  221.4 90.4 all-reduce.13
  314.8 32.4 all-reduce.15
  363.2 90.4 all-reduce.17
  456.1 32.4 all-reduce.19
where the time goes:
time: 581 us; the launch traced here: 578 us
  waiting for transfers between devices  316 us (54%)
  matrix products  217 us (37%)
  local copies, waits for them, and re-layouts  19.5 us (3%)
  between operations  13.5 us (2%)
  other arithmetic  10.9 us (2%)
    psum x3, waiting for transfers between devices, per_device(): lax.psum(partial_sum.astype(jnp.bfloat16), 'row').astype(jnp.float32)  242 us
    dot_general x4, matrix products, per_device(): lax.dot_general(grad_here, rates[step - 1], (((1,), (1,)), ((), ())), pre...  169 us
    psum x4, waiting for transfers between devices, spread(): return lax.psum(block, axis)  74.2 us
    dot_general x3, matrix products, per_device(): lax.dot_general(weights, grad_here, (((0,), (0,)), ((), ())), preferred_e...  47.2 us
  transfers between devices with their start and end apart: 7, of which 7 were waited for; matrix products, arithmetic and copies ran while one was open for 15% of the time, Pallas kernels for 0%

commit v1 on v0

v1 whole, which is shorter than its diff:
```python
import jax
import jax.numpy as jnp
from jax import lax
from jax.sharding import PartitionSpec as P

STEPS = 4


def per_device(rows, cols, weights, rates):
    chunk = weights.shape[1] // rows
    row_index = lax.axis_index("row")
    exchange = [(r * cols + c, c * rows + r) for r in range(rows) for c in range(cols)]
    own = lax.dynamic_slice_in_dim(rates, row_index * chunk, chunk, 1).astype(jnp.float32)

    def local_grad(adjoint, step):
        return (adjoint * (1.0 - own[step] * own[step])).astype(jnp.bfloat16)

    def spread(piece):
        moved = lax.ppermute(piece, ("row", "col"), exchange)
        return lax.all_gather(moved, "col", axis=0, tiled=True)

    grad = spread(local_grad(own[STEPS] - own[0], STEPS))
    grads = [grad]
    for step in range(STEPS, 1, -1):
        partial_sum = lax.dot_general(
            weights, grad, (((0,), (0,)), ((), ())), preferred_element_type=jnp.float32
        ).astype(jnp.bfloat16)
        split = partial_sum.reshape(rows, chunk, -1)
        split = lax.all_to_all(split, "row", split_axis=0, concat_axis=0)
        adjoint = jnp.sum(split.astype(jnp.float32), axis=0)
        grad = spread(local_grad(adjoint.astype(jnp.float32), step - 1))
        grads.append(grad)
    stacked = jnp.concatenate(grads, axis=1)
    previous = jnp.concatenate([rates[step - 1] for step in range(STEPS, 0, -1)], axis=1)
    return lax.dot_general(
        stacked, previous, (((1,), (1,)), ((), ())), preferred_element_type=jnp.float32
    ).astype(jnp.bfloat16)


def solution(mesh):
    rows, cols = mesh.shape["row"], mesh.shape["col"]

    def body(weights, rates):
        return per_device(rows, cols, weights, rates)

    return jax.shard_map(
        body, mesh=mesh, in_specs=(P("row", "col"), P(None, "col", None)),
        out_specs=P("row", "col"), check_vma=False
    )
```

time: 581 us -> 287 us (0.49)
  waiting for transfers between devices: 316 us -> 22.3 us
  blocking collectives: 0 us -> 169 us
  matrix products: 217 us -> 71.7 us
  starting transfers between devices: 0.66 us -> 16.6 us
  between operations: 13.5 us -> 0.19 us
  local copies, waits for them, and re-layouts: 19.5 us -> 6.37 us
  other arithmetic: 10.9 us -> 1.05 us
    psum x7 -> x0, waiting for transfers between devices: 316 us -> none  [the longest x3 242 us: per_device(): lax.psum(partial_sum.astype(jnp.bfloat16), 'row').astype(jnp.float32)]
    dot_general x7 -> x4, matrix products: 217 us -> 71.7 us  [the longest x3 45.7 us: per_device(): lax.dot_general(weights, grad, (((0,), (0,)), ((), ())), preferred_elemen...]
    all_to_all x0 -> x3, blocking collectives: none -> 118 us  [per_device(): split = lax.all_to_all(split, 'row', split_axis=0, concat_axis=0)]
    all_gather x0 -> x4, blocking collectives: none -> 51.2 us  [spread(): return lax.all_gather(moved, 'col', axis=0, tiled=True)]
    ppermute x0 -> x4, waiting for transfers between devices: none -> 22.3 us  [spread(): moved = lax.ppermute(piece, ('row', 'col'), exchange)]
    ppermute x0 -> x4, starting transfers between devices: none -> 16.6 us  [spread(): moved = lax.ppermute(piece, ('row', 'col'), exchange)]
    select_n x4 -> x0, other arithmetic: 10.9 us -> none  [spread(): jnp.where(lax.axis_index(axis) == owner, block, jnp.zeros_like(block))]
    unnamed x1 -> x13, local copies, waits for them, and re-layouts: 10.6 us -> 0.65 us
  transfers between devices with their start and end apart: 7 -> 4, of which waited for: 7 -> 4; matrix products, arithmetic and copies ran while one was open for 15% -> 1% of each run, Pallas kernels for 0% -> 0%
where the time goes in v1:
time: 287 us
  blocking collectives  169 us (59%)
  matrix products  71.7 us (25%)
  waiting for transfers between devices  22.3 us (8%)
  starting transfers between devices  16.6 us (6%)
  local copies, waits for them, and re-layouts  6.37 us (2%)
    all_to_all x3, blocking collectives, per_device(): split = lax.all_to_all(split, 'row', split_axis=0, concat_axis=0)  118 us
    all_gather x4, blocking collectives, spread(): return lax.all_gather(moved, 'col', axis=0, tiled=True)  51.2 us
    dot_general x3, matrix products, per_device(): lax.dot_general(weights, grad, (((0,), (0,)), ((), ())), preferred_elemen...  45.7 us
    dot_general x1, matrix products, per_device(): lax.dot_general(stacked, previous, (((1,), (1,)), ((), ())), preferred_el...  26.1 us
    ppermute x4, waiting for transfers between devices, spread(): moved = lax.ppermute(piece, ('row', 'col'), exchange)  22.3 us
    ppermute x4, starting transfers between devices, spread(): moved = lax.ppermute(piece, ('row', 'col'), exchange)  16.6 us
  transfers between devices with their start and end apart: 4, of which 4 were waited for; matrix products, arithmetic and copies ran while one was open for 1% of the time, Pallas kernels for 0%

profile of v1, /device:TPU:7, one launch (start us, length us, event | category | flops | bytes accessed | tf_op | source)
XLA Modules:
  0.0 287.1 jit_solution(2150474279437430644)
XLA Ops:
  0.0 1.3 constant_dynamic-slice_fusion
  1.3 0.6 copy.13
  1.9 0.2 convert_element_type.48
  2.1 0.1 fusion.28
  2.2 5.1 %collective-permute-start = (bf16[768,128]{0,1:T(8,128)(2,1)S(1)}, bf16[768,128]{0,1:T(8,128)(2,1)S(1)}, u32[]{:S(2)}, u32[]{:S(2)}) collective-permute-start(bf16[768,128]{0,1:T(8,128)(2,1)S(1)} %fusion.28), channel_id=1, source_target_pairs={{0,0},{1,8},{2,16},{3,24},{4,1},{5,9},{6,17},{7,25},{8,2},{9,10},{... | collective-permute-start | bytes 589832 | tf_op jit(solution)/shard_map/ppermute | solution.py:19
  7.3 6.5 %collective-permute-done = bf16[768,128]{0,1:T(8,128)(2,1)S(1)} collective-permute-done((bf16[768,128]{0,1:T(8,128)(2,1)S(1)}, bf16[768,128]{0,1:T(8,128)(2,1)S(1)}, u32[]{:S(2)}, u32[]{:S(2)}) %collective-permute-start) | collective-permute-done | bytes 196640 | tf_op jit(solution)/shard_map/ppermute | solution.py:19
  13.8 11.7 %all_gather.12 = bf16[3072,128]{0,1:T(8,128)(2,1)S(1)} all-gather(bf16[768,128]{0,1:T(8,128)(2,1)S(1)} %collective-permute-done), channel_id=1, replica_groups=mesh['row'=8,'col'=4] {'col'}, dimensions={0}, use_global_device_ids=true | all-gather | bytes 983040 | tf_op jit(solution)/shard_map/all_gather | solution.py:20
  25.5 14.9 %convolution_convert_fusion.3 = bf16[128,6144]{1,0:T(8,128)(2,1)S(1)} fusion(bf16[3072,128]{0,1:T(8,128)(2,1)S(1)} %all_gather.12, bf16[3072,6144]{1,0:T(8,128)(2,1)} %param.2), kind=kOutput, calls=%fused_computation.3 | convolution fusion | flops 4832624640 | bytes 40108032 | tf_op jit(solution)/shard_map/dot_general | solution.py:25
  40.4 0.1 copy.22
  40.6 40.1 %all_to_all.15 = bf16[8,768,128]{1,2,0:T(8,128)(2,1)S(1)} all-to-all(bf16[8,768,128]{1,2,0:T(8,128)(2,1)S(1)} %bitcast.54), channel_id=1, replica_groups=mesh['row'=8,'col'=4] {'row'}, dimensions={0} | all-to-all | bytes 3145728 | tf_op jit(solution)/shard_map/all_to_all | solution.py:29
  80.7 0.2 convert_reduce_fusion.2
  80.9 3.4 %collective-permute-start.1 = (bf16[768,128]{0,1:T(8,128)(2,1)S(1)}, bf16[768,128]{0,1:T(8,128)(2,1)S(1)}, u32[]{:S(2)}, u32[]{:S(2)}) collective-permute-start(bf16[768,128]{0,1:T(8,128)(2,1)S(1)} %fusion.25), channel_id=1, source_target_pairs={{0,0},{1,8},{2,16},{3,24},{4,1},{5,9},{6,17},{7,25},{8,2},{9,10},{... | collective-permute-start | bytes 589832 | tf_op jit(solution)/shard_map/ppermute | solution.py:19
  84.3 6.4 %collective-permute-done.1 = bf16[768,128]{0,1:T(8,128)(2,1)S(1)} collective-permute-done((bf16[768,128]{0,1:T(8,128)(2,1)S(1)}, bf16[768,128]{0,1:T(8,128)(2,1)S(1)}, u32[]{:S(2)}, u32[]{:S(2)}) %collective-permute-start.1) | collective-permute-done | bytes 196640 | tf_op jit(solution)/shard_map/ppermute | solution.py:19
  90.7 12.8 %all_gather.13 = bf16[3072,128]{0,1:T(8,128)(2,1)S(1)} all-gather(bf16[768,128]{0,1:T(8,128)(2,1)S(1)} %collective-permute-done.1), channel_id=1, replica_groups=mesh['row'=8,'col'=4] {'col'}, dimensions={0}, use_global_device_ids=true | all-gather | bytes 983040 | tf_op jit(solution)/shard_map/all_gather | solution.py:20
  103.6 14.9 %convolution_convert_fusion.2 = bf16[128,6144]{1,0:T(8,128)(2,1)S(1)} fusion(bf16[3072,128]{0,1:T(8,128)(2,1)S(1)} %all_gather.13, bf16[3072,6144]{1,0:T(8,128)(2,1)} %param.2), kind=kOutput, calls=%fused_computation.2 | convolution fusion | flops 4832624640 | bytes 40108032 | tf_op jit(solution)/shard_map/dot_general | solution.py:25
  118.5 0.1 copy.21
  118.6 38.9 %all_to_all.16 = bf16[8,768,128]{1,2,0:T(8,128)(2,1)S(1)} all-to-all(bf16[8,768,128]{1,2,0:T(8,128)(2,1)S(1)} %bitcast.55), channel_id=1, replica_groups=mesh['row'=8,'col'=4] {'row'}, dimensions={0} | all-to-all | bytes 3145728 | tf_op jit(solution)/shard_map/all_to_all | solution.py:29
  157.5 0.2 convert_reduce_fusion.1
  157.7 0.1 fusion.21
  157.8 4.1 %collective-permute-start.2 = (bf16[768,128]{0,1:T(8,128)(2,1)S(1)}, bf16[768,128]{0,1:T(8,128)(2,1)S(1)}, u32[]{:S(2)}, u32[]{:S(2)}) collective-permute-start(bf16[768,128]{0,1:T(8,128)(2,1)S(1)} %fusion.21), channel_id=1, source_target_pairs={{0,0},{1,8},{2,16},{3,24},{4,1},{5,9},{6,17},{7,25},{8,2},{9,10},{... | collective-permute-start | bytes 589832 | tf_op jit(solution)/shard_map/ppermute | solution.py:19
  161.8 6.2 %collective-permute-done.2 = bf16[768,128]{0,1:T(8,128)(2,1)S(1)} collective-permute-done((bf16[768,128]{0,1:T(8,128)(2,1)S(1)}, bf16[768,128]{0,1:T(8,128)(2,1)S(1)}, u32[]{:S(2)}, u32[]{:S(2)}) %collective-permute-start.2) | collective-permute-done | bytes 196640 | tf_op jit(solution)/shard_map/ppermute | solution.py:19
  168.1 13.6 %all_gather.14 = bf16[3072,128]{0,1:T(8,128)(2,1)} all-gather(bf16[768,128]{0,1:T(8,128)(2,1)S(1)} %collective-permute-done.2), channel_id=1, replica_groups=mesh['row'=8,'col'=4] {'col'}, dimensions={0}, use_global_device_ids=true | all-gather | bytes 983040 | tf_op jit(solution)/shard_map/all_gather | solution.py:20
  181.7 15.9 %convolution_convert_fusion.1 = bf16[128,6144]{1,0:T(8,128)(2,1)} fusion(bf16[3072,128]{0,1:T(8,128)(2,1)} %all_gather.14, bf16[3072,6144]{1,0:T(8,128)(2,1)} %param.2), kind=kOutput, calls=%fused_computation.1 | convolution fusion | flops 4832624640 | bytes 40108032 | tf_op jit(solution)/shard_map/dot_general | solution.py:25
  197.6 1.5 copy.20
  199.1 38.6 %all_to_all.17 = bf16[8,768,128]{1,2,0:T(8,128)(2,1)S(1)} all-to-all(bf16[8,768,128]{1,2,0:T(8,128)(2,1)S(1)} %bitcast.56), channel_id=1, replica_groups=mesh['row'=8,'col'=4] {'row'}, dimensions={0} | all-to-all | bytes 3145728 | tf_op jit(solution)/shard_map/all_to_all | solution.py:29
  237.7 0.2 convert_reduce_fusion
  237.9 0.1 fusion.17
  238.0 4.0 %collective-permute-start.3 = (bf16[768,128]{0,1:T(8,128)(2,1)S(1)}, bf16[768,128]{0,1:T(8,128)(2,1)S(1)}, u32[]{:S(2)}, u32[]{:S(2)}) collective-permute-start(bf16[768,128]{0,1:T(8,128)(2,1)S(1)} %fusion.17), channel_id=1, source_target_pairs={{0,0},{1,8},{2,16},{3,24},{4,1},{5,9},{6,17},{7,25},{8,2},{9,10},{... | collective-permute-start | bytes 589832 | tf_op jit(solution)/shard_map/ppermute | solution.py:19
  242.0 2.7 slice_bitcast_fusion.3
  244.7 3.2 %collective-permute-done.3 = bf16[768,128]{0,1:T(8,128)(2,1)S(1)} collective-permute-done((bf16[768,128]{0,1:T(8,128)(2,1)S(1)}, bf16[768,128]{0,1:T(8,128)(2,1)S(1)}, u32[]{:S(2)}, u32[]{:S(2)}) %collective-permute-start.3) | collective-permute-done | bytes 196640 | tf_op jit(solution)/shard_map/ppermute | solution.py:19
  247.9 13.1 %all_gather.15 = bf16[3072,128]{0,1:T(8,128)(2,1)S(1)} all-gather(bf16[768,128]{0,1:T(8,128)(2,1)S(1)} %collective-permute-done.3), channel_id=1, replica_groups=mesh['row'=8,'col'=4] {'col'}, dimensions={0}, use_global_device_ids=true | all-gather | bytes 983040 | tf_op jit(solution)/shard_map/all_gather | solution.py:20
  261.0 26.1 %convolution_convert_fusion = bf16[3072,6144]{1,0:T(8,128)(2,1)} fusion(bf16[6144,128]{1,0:T(8,128)(2,1)} %get-tuple-element.7, bf16[6144,128]{1,0:T(8,128)(2,1)} %get-tuple-element.8, bf16[6144,128]{1,0:T(8,128)(2,1)} %get-tuple-element.6, bf16[6144,128]{1,0:T(8,128)(2,1)} %get-tuple-element.5, bf16[3072,128]{0,1:T(8,128)(2,1)S(1)} %all_gather.15, ...), kind=kOutput, calls=%fused_computation | convolution fusion | flops 19383975936 | bytes 47185920 | tf_op jit(solution)/shard_map/dot_general | solution.py:35
  (14 shorter events, 0.1 us)
Async XLA Ops:
  2.2 11.7 %collective-permute-start = (bf16[768,128]{0,1:T(8,128)(2,1)S(1)}, bf16[768,128]{0,1:T(8,128)(2,1)S(1)}, u32[]{:S(2)}, u32[]{:S(2)}) collective-permute-start(bf16[768,128]{0,1:T(8,128)(2,1)S(1)} %fusion.28), channel_id=1, source_target_pairs={{0,0},{1,8},{2,16},{3,24},{4,1},{5,9},{6,17},{7,25},{8,2},{9,10},{... | collective-permute-start | bytes 589832 | tf_op jit(solution)/shard_map/ppermute | solution.py:19
  25.5 14.9 %copy-start = (bf16[3072,128]{0,1:T(8,128)(2,1)}, bf16[3072,128]{0,1:T(8,128)(2,1)S(1)}, u32[]{:S(2)}) copy-start(bf16[3072,128]{0,1:T(8,128)(2,1)S(1)} %all_gather.12) | copy-start | bytes 2359300
  80.9 9.8 %collective-permute-start.1 = (bf16[768,128]{0,1:T(8,128)(2,1)S(1)}, bf16[768,128]{0,1:T(8,128)(2,1)S(1)}, u32[]{:S(2)}, u32[]{:S(2)}) collective-permute-start(bf16[768,128]{0,1:T(8,128)(2,1)S(1)} %fusion.25), channel_id=1, source_target_pairs={{0,0},{1,8},{2,16},{3,24},{4,1},{5,9},{6,17},{7,25},{8,2},{9,10},{... | collective-permute-start | bytes 589832 | tf_op jit(solution)/shard_map/ppermute | solution.py:19
  103.6 14.9 %copy-start.2 = (bf16[3072,128]{0,1:T(8,128)(2,1)}, bf16[3072,128]{0,1:T(8,128)(2,1)S(1)}, u32[]{:S(2)}) copy-start(bf16[3072,128]{0,1:T(8,128)(2,1)S(1)} %all_gather.13) | copy-start | bytes 2359300
  157.8 10.3 %collective-permute-start.2 = (bf16[768,128]{0,1:T(8,128)(2,1)S(1)}, bf16[768,128]{0,1:T(8,128)(2,1)S(1)}, u32[]{:S(2)}, u32[]{:S(2)}) collective-permute-start(bf16[768,128]{0,1:T(8,128)(2,1)S(1)} %fusion.21), channel_id=1, source_target_pairs={{0,0},{1,8},{2,16},{3,24},{4,1},{5,9},{6,17},{7,25},{8,2},{9,10},{... | collective-permute-start | bytes 589832 | tf_op jit(solution)/shard_map/ppermute | solution.py:19
  168.1 73.9 %slice-start = ((s8[7864320]{0:T(1024)(128)(4,1)}), s8[4194304]{0:T(1024)(128)(4,1)S(1)}, s32[]{:S(2)}) async-start(s8[7864320]{0:T(1024)(128)(4,1)} %bitcast.49), calls=%async_computation.3 | async-start | bytes 8388608
  181.7 60.3 %slice-start.1 = ((s8[7864320]{0:T(1024)(128)(4,1)}), s8[3670016]{0:T(1024)(128)(4,1)S(1)}, s32[]{:S(2)}) async-start(s8[7864320]{0:T(1024)(128)(4,1)} %bitcast.49), calls=%async_computation.4 | async-start | bytes 7340032
  237.9 23.1 %copy-start.1 = (bf16[3072,128]{0,1:T(8,128)(2,1)S(1)}, bf16[3072,128]{0,1:T(8,128)(2,1)}, u32[]{:S(2)}) copy-start(bf16[3072,128]{0,1:T(8,128)(2,1)} %copy-done) | copy-start | bytes 2359300
  238.0 23.1 %copy-start.3 = (bf16[3072,128]{0,1:T(8,128)(2,1)S(1)}, bf16[3072,128]{0,1:T(8,128)(2,1)}, u32[]{:S(2)}) copy-start(bf16[3072,128]{0,1:T(8,128)(2,1)} %copy-done.2) | copy-start | bytes 2359300
  238.0 9.9 %collective-permute-start.3 = (bf16[768,128]{0,1:T(8,128)(2,1)S(1)}, bf16[768,128]{0,1:T(8,128)(2,1)S(1)}, u32[]{:S(2)}, u32[]{:S(2)}) collective-permute-start(bf16[768,128]{0,1:T(8,128)(2,1)S(1)} %fusion.17), channel_id=1, source_target_pairs={{0,0},{1,8},{2,16},{3,24},{4,1},{5,9},{6,17},{7,25},{8,2},{9,10},{... | collective-permute-start | bytes 589832 | tf_op jit(solution)/shard_map/ppermute | solution.py:19

commit v2 on v1

--- a/solution.py
+++ b/solution.py
@@ -1,9 +1,84 @@
+import functools
+
 import jax
 import jax.numpy as jnp
 from jax import lax
+from jax.experimental import pallas as pl
+from jax.experimental.pallas import tpu as pltpu
 from jax.sharding import PartitionSpec as P
 
 STEPS = 4
+
+
+def exchange_kernel(
+    rows, part_ref, own_ref, out_ref,
+    halves, merged, landed, total, pair_send, pair_recv, send_sem, recv_sem,
+):
+    row, col = lax.axis_index("row"), lax.axis_index("col")
+    mesh_ids = pl.DeviceIdType.MESH
+    groups, parity, group = rows // 2, row % 2, row // 2
+    pair = row + 1 - 2 * parity
+    order = list(range(1, groups)) + [0]
+    paired, sums = {}, {}
+
+    barrier = pltpu.get_barrier_semaphore()
+    for peer in [pair] + [2 * ((group + turn) % groups) + parity for turn in range(1, groups)]:
+        pl.semaphore_signal(barrier, inc=1, device_id=(peer, col), device_id_type=mesh_ids)
+    pl.semaphore_wait(barrier, groups)
+
+    for turn in order:
+        owner = 2 * ((group + turn) % groups)
+        paired[turn] = pltpu.make_async_remote_copy(
+            src_ref=part_ref.at[owner + 1 - parity], dst_ref=halves.at[turn],
+            send_sem=pair_send.at[turn], recv_sem=pair_recv.at[turn],
+            device_id=(pair, col), device_id_type=mesh_ids,
+        )
+        paired[turn].start()
+    for turn in order:
+        owner = 2 * ((group + turn) % groups) + parity
+        paired[turn].wait_recv()
+        both = part_ref[owner].astype(jnp.float32) + halves[turn].astype(jnp.float32)
+        if turn:
+            merged[turn] = both.astype(jnp.bfloat16)
+            sums[turn] = pltpu.make_async_remote_copy(
+                src_ref=merged.at[turn], dst_ref=landed.at[turn],
+                send_sem=send_sem.at[turn], recv_sem=recv_sem.at[turn],
+                device_id=(owner, col), device_id_type=mesh_ids,
+            )
+            sums[turn].start()
+        else:
+            total[...] = both
+    for turn in sums:
+        sums[turn].wait_recv()
+        total[...] += landed[turn].astype(jnp.float32)
+    own = own_ref[...].astype(jnp.float32)
+    out_ref[...] = (total[...] * (1.0 - own * own)).astype(jnp.bfloat16)
+    for copy in list(paired.values()) + list(sums.values()):
+        copy.wait_send()
+
+
+def exchange_sum(rows, parts, own):
+    chunk, trials = own.shape
+    vmem = pl.BlockSpec(memory_space=pltpu.VMEM)
+    return pl.pallas_call(
+        functools.partial(exchange_kernel, rows),
+        out_shape=jax.ShapeDtypeStruct((chunk, trials), jnp.bfloat16),
+        in_specs=[vmem, vmem],
+        out_specs=vmem,
+        scratch_shapes=[
+            pltpu.VMEM((rows // 2, chunk, trials), jnp.bfloat16),
+            pltpu.VMEM((rows // 2, chunk, trials), jnp.bfloat16),
+            pltpu.VMEM((rows // 2, chunk, trials), jnp.bfloat16),
+            pltpu.VMEM((chunk, trials), jnp.float32),
+            pltpu.SemaphoreType.DMA((rows // 2,)),
+            pltpu.SemaphoreType.DMA((rows // 2,)),
+            pltpu.SemaphoreType.DMA((rows // 2,)),
+            pltpu.SemaphoreType.DMA((rows // 2,)),
+        ],
+        compiler_params=pltpu.CompilerParams(
+            collective_id=0, has_side_effects=True, vmem_limit_bytes=24 * 1024 * 1024
+        ),
+    )(parts, own)
 
 
 def per_device(rows, cols, weights, rates):
@@ -26,9 +101,8 @@
             weights, grad, (((0,), (0,)), ((), ())), preferred_element_type=jnp.float32
         ).astype(jnp.bfloat16)
         split = partial_sum.reshape(rows, chunk, -1)
-        split = lax.all_to_all(split, "row", split_axis=0, concat_axis=0)
-        adjoint = jnp.sum(split.astype(jnp.float32), axis=0)
-        grad = spread(local_grad(adjoint.astype(jnp.float32), step - 1))
+        own_rates = lax.dynamic_slice_in_dim(rates[step - 1], row_index * chunk, chunk, 0)
+        grad = spread(exchange_sum(rows, split, own_rates))
         grads.append(grad)
     stacked = jnp.concatenate(grads, axis=1)
     previous = jnp.concatenate([rates[step - 1] for step in range(STEPS, 0, -1)], axis=1)

time: 287 us -> 247 us (0.86)
  blocking collectives: 169 us -> 47.2 us
  Pallas kernels: 0 us -> 77.8 us
  local copies, waits for them, and re-layouts: 6.37 us -> 13.2 us
    all_to_all x3 -> x0, blocking collectives: 118 us -> none  [per_device(): split = lax.all_to_all(split, 'row', split_axis=0, concat_axis=0)]
    pallas_call x0 -> x3, Pallas kernels: none -> 77.8 us  [exchange_sum(): pl.pallas_call(functools.partial(exchange_kernel, rows), out_shape=jax.Sh...]
    slice x0 -> x1, local copies, waits for them, and re-layouts: none -> 5.82 us  [per_device(): rates[step - 1]]
    all_gather x4, blocking collectives: 51.2 us -> 47.2 us  [spread(): return lax.all_gather(moved, 'col', axis=0, tiled=True)]
  transfers between devices with their start and end apart: 4 -> 4, of which waited for: 4 -> 4; matrix products, arithmetic and copies ran while one was open for 1% -> 3% of each run, Pallas kernels for 0% -> 0%
where the time goes in v2:
time: 247 us
  Pallas kernels  77.8 us (31%)
  matrix products  70.6 us (29%)
  blocking collectives  47.2 us (19%)
  waiting for transfers between devices  20.5 us (8%)
  starting transfers between devices  15.8 us (6%)
  local copies, waits for them, and re-layouts  13.2 us (5%)
    pallas_call x3, Pallas kernels, exchange_sum(): pl.pallas_call(functools.partial(exchange_kernel, rows), out_shape=jax.Sh...  77.8 us
    all_gather x4, blocking collectives, spread(): return lax.all_gather(moved, 'col', axis=0, tiled=True)  47.2 us
    dot_general x3, matrix products, per_device(): lax.dot_general(weights, grad, (((0,), (0,)), ((), ())), preferred_elemen...  44.1 us
    dot_general x1, matrix products, per_device(): lax.dot_general(stacked, previous, (((1,), (1,)), ((), ())), preferred_el...  26.5 us
    ppermute x4, waiting for transfers between devices, spread(): moved = lax.ppermute(piece, ('row', 'col'), exchange)  20.5 us
    ppermute x4, starting transfers between devices, spread(): moved = lax.ppermute(piece, ('row', 'col'), exchange)  15.8 us
    slice x1, local copies, waits for them, and re-layouts, per_device(): rates[step - 1]  5.82 us
  transfers between devices with their start and end apart: 4, of which 4 were waited for; matrix products, arithmetic and copies ran while one was open for 3% of the time, Pallas kernels for 0%

profile of v2, /device:TPU:7, one launch (start us, length us, event | category | flops | bytes accessed | tf_op | source)
XLA Modules:
  0.0 246.7 jit_solution(13382131332383076595)
XLA Ops:
  0.0 1.3 dynamic-slice_convert_fusion
  1.3 0.1 fusion.19
  1.4 5.1 %collective-permute-start = (bf16[768,128]{1,0:T(8,128)(2,1)S(1)}, bf16[768,128]{1,0:T(8,128)(2,1)S(1)}, u32[]{:S(2)}, u32[]{:S(2)}) collective-permute-start(bf16[768,128]{1,0:T(8,128)(2,1)S(1)} %fusion.19), channel_id=1, source_target_pairs={{0,0},{1,8},{2,16},{3,24},{4,1},{5,9},{6,17},{7,25},{8,2},{9,10},{... | collective-permute-start | bytes 589832 | tf_op jit(solution)/shard_map/ppermute | solution.py:94
  6.6 5.8 %fusion.21 = (bf16[1,6144,128]{2,1,0:T(8,128)(2,1)}, bf16[6144,128]{1,0:T(8,128)(2,1)}, bf16[6144,128]{1,0:T(8,128)(2,1)}, bf16[6144,128]{1,0:T(8,128)(2,1)}, bf...) fusion(bf16[5,6144,128]{2,1,0:T(8,128)(2,1)} %param.3), kind=kLoop, calls=%fused_computation.34 | loop fusion | bytes 17301504 | tf_op jit(solution)/shard_map/slice | solution.py:104
  12.4 0.7 collective-permute-done
  13.1 11.7 %all_gather.12 = bf16[3072,128]{1,0:T(8,128)(2,1)S(1)} all-gather(bf16[768,128]{1,0:T(8,128)(2,1)S(1)} %collective-permute-done), channel_id=1, replica_groups=mesh['row'=8,'col'=4] {'col'}, dimensions={0}, use_global_device_ids=true | all-gather | bytes 983040 | tf_op jit(solution)/shard_map/all_gather | solution.py:95
  24.8 0.0 copy-start
  24.8 1.0 copy-done
  25.7 14.7 %fusion = bf16[6144,128]{0,1:T(8,128)(2,1)S(1)} fusion(bf16[3072,128]{1,0:T(8,128)(2,1)S(1)} %all_gather.12, bf16[3072,6144]{1,0:T(8,128)(2,1)} %param.2), kind=kOutput, calls=%fused_computation.4 | convolution fusion | flops 4832624640 | bytes 40108032 | tf_op jit(solution)/shard_map/dot_general | solution.py:100
  40.5 0.9 copy.3
  41.4 26.3 %shard_map.28 = bf16[768,128]{1,0:T(8,128)(2,1)S(1)} custom-call(bf16[8,768,128]{2,1,0:T(8,128)(2,1)S(1)} %bitcast.31, bf16[768,128]{1,0:T(8,128)(2,1)S(1)} %dynamic-slice_bitcast_fusion.2.own_ref), custom_call_target="tpu_custom_call" | custom-call | tf_op jit(solution)/shard_map/pallas_call | solution.py:63
  67.7 3.2 %collective-permute-start.1 = (bf16[768,128]{1,0:T(8,128)(2,1)S(1)}, bf16[768,128]{1,0:T(8,128)(2,1)S(1)}, u32[]{:S(2)}, u32[]{:S(2)}) collective-permute-start(bf16[768,128]{1,0:T(8,128)(2,1)S(1)} %shard_map.28), channel_id=1, source_target_pairs={{0,0},{1,8},{2,16},{3,24},{4,1},{5,9},{6,17},{7,25},{8,2},{9,10},{... | collective-permute-start | bytes 589832 | tf_op jit(solution)/shard_map/ppermute | solution.py:94
  70.9 0.9 dynamic-slice_bitcast_fusion.1.own_ref
  71.8 6.5 %collective-permute-done.1 = bf16[768,128]{1,0:T(8,128)(2,1)S(1)} collective-permute-done((bf16[768,128]{1,0:T(8,128)(2,1)S(1)}, bf16[768,128]{1,0:T(8,128)(2,1)S(1)}, u32[]{:S(2)}, u32[]{:S(2)}) %collective-permute-start.1) | collective-permute-done | bytes 196640 | tf_op jit(solution)/shard_map/ppermute | solution.py:94
  78.4 11.6 %all_gather.13 = bf16[3072,128]{1,0:T(8,128)(2,1)S(1)} all-gather(bf16[768,128]{1,0:T(8,128)(2,1)S(1)} %collective-permute-done.1), channel_id=1, replica_groups=mesh['row'=8,'col'=4] {'col'}, dimensions={0}, use_global_device_ids=true | all-gather | bytes 983040 | tf_op jit(solution)/shard_map/all_gather | solution.py:95
  90.0 0.0 copy-start.1
  90.0 0.9 copy-done.1
  90.8 14.7 %fusion.1 = bf16[6144,128]{0,1:T(8,128)(2,1)S(1)} fusion(bf16[3072,128]{1,0:T(8,128)(2,1)S(1)} %all_gather.13, bf16[3072,6144]{1,0:T(8,128)(2,1)} %param.2), kind=kOutput, calls=%fused_computation.5 | convolution fusion | flops 4832624640 | bytes 40108032 | tf_op jit(solution)/shard_map/dot_general | solution.py:100
  105.6 0.9 copy.4
  106.5 25.7 %shard_map.29 = bf16[768,128]{1,0:T(8,128)(2,1)S(1)} custom-call(bf16[8,768,128]{2,1,0:T(8,128)(2,1)S(1)} %bitcast.32, bf16[768,128]{1,0:T(8,128)(2,1)S(1)} %dynamic-slice_bitcast_fusion.1.own_ref), custom_call_target="tpu_custom_call" | custom-call | tf_op jit(solution)/shard_map/pallas_call | solution.py:63
  132.2 3.8 %collective-permute-start.2 = (bf16[768,128]{1,0:T(8,128)(2,1)S(1)}, bf16[768,128]{1,0:T(8,128)(2,1)S(1)}, u32[]{:S(2)}, u32[]{:S(2)}) collective-permute-start(bf16[768,128]{1,0:T(8,128)(2,1)S(1)} %shard_map.29), channel_id=1, source_target_pairs={{0,0},{1,8},{2,16},{3,24},{4,1},{5,9},{6,17},{7,25},{8,2},{9,10},{... | collective-permute-start | bytes 589832 | tf_op jit(solution)/shard_map/ppermute | solution.py:94
  136.0 0.9 dynamic-slice_bitcast_fusion.own_ref
  136.9 6.1 %collective-permute-done.2 = bf16[768,128]{1,0:T(8,128)(2,1)S(1)} collective-permute-done((bf16[768,128]{1,0:T(8,128)(2,1)S(1)}, bf16[768,128]{1,0:T(8,128)(2,1)S(1)}, u32[]{:S(2)}, u32[]{:S(2)}) %collective-permute-start.2) | collective-permute-done | bytes 196640 | tf_op jit(solution)/shard_map/ppermute | solution.py:94
  143.0 12.1 %all_gather.14 = bf16[3072,128]{1,0:T(8,128)(2,1)S(1)} all-gather(bf16[768,128]{1,0:T(8,128)(2,1)S(1)} %collective-permute-done.2), channel_id=1, replica_groups=mesh['row'=8,'col'=4] {'col'}, dimensions={0}, use_global_device_ids=true | all-gather | bytes 983040 | tf_op jit(solution)/shard_map/all_gather | solution.py:95
  155.1 0.9 copy-done.2
  156.0 14.7 %fusion.2 = bf16[6144,128]{0,1:T(8,128)(2,1)S(1)} fusion(bf16[3072,128]{1,0:T(8,128)(2,1)S(1)} %all_gather.14, bf16[3072,6144]{1,0:T(8,128)(2,1)} %param.2), kind=kOutput, calls=%fused_computation.6 | convolution fusion | flops 4832624640 | bytes 40108032 | tf_op jit(solution)/shard_map/dot_general | solution.py:100
  170.7 0.9 copy.5
  171.6 25.8 %shard_map.30 = bf16[768,128]{1,0:T(8,128)(2,1)S(1)} custom-call(bf16[8,768,128]{2,1,0:T(8,128)(2,1)S(1)} %bitcast.33, bf16[768,128]{1,0:T(8,128)(2,1)S(1)} %dynamic-slice_bitcast_fusion.own_ref), custom_call_target="tpu_custom_call" | custom-call | tf_op jit(solution)/shard_map/pallas_call | solution.py:63
  197.4 3.7 %collective-permute-start.3 = (bf16[768,128]{1,0:T(8,128)(2,1)S(1)}, bf16[768,128]{1,0:T(8,128)(2,1)S(1)}, u32[]{:S(2)}, u32[]{:S(2)}) collective-permute-start(bf16[768,128]{1,0:T(8,128)(2,1)S(1)} %shard_map.30), channel_id=1, source_target_pairs={{0,0},{1,8},{2,16},{3,24},{4,1},{5,9},{6,17},{7,25},{8,2},{9,10},{... | collective-permute-start | bytes 589832 | tf_op jit(solution)/shard_map/ppermute | solution.py:94
  201.1 7.2 %collective-permute-done.3 = bf16[768,128]{1,0:T(8,128)(2,1)S(1)} collective-permute-done((bf16[768,128]{1,0:T(8,128)(2,1)S(1)}, bf16[768,128]{1,0:T(8,128)(2,1)S(1)}, u32[]{:S(2)}, u32[]{:S(2)}) %collective-permute-start.3) | collective-permute-done | bytes 196640 | tf_op jit(solution)/shard_map/ppermute | solution.py:94
  208.3 11.9 %all_gather.15 = bf16[3072,128]{1,0:T(8,128)(2,1)S(1)} all-gather(bf16[768,128]{1,0:T(8,128)(2,1)S(1)} %collective-permute-done.3), channel_id=1, replica_groups=mesh['row'=8,'col'=4] {'col'}, dimensions={0}, use_global_device_ids=true | all-gather | bytes 983040 | tf_op jit(solution)/shard_map/all_gather | solution.py:95
  220.2 26.5 %convolution_convert_fusion = bf16[3072,6144]{1,0:T(8,128)(2,1)} fusion(bf16[6144,128]{1,0:T(8,128)(2,1)} %get-tuple-element.11, bf16[6144,128]{1,0:T(8,128)(2,1)} %get-tuple-element.8, bf16[6144,128]{1,0:T(8,128)(2,1)} %get-tuple-element.7, bf16[6144,128]{1,0:T(8,128)(2,1)} %get-tuple-element.6, bf16[3072,128]{1,0:T(8,128)(2,1)S(1)} %all_gather.15, ...), kind=kOutput, calls=%fused_computation | convolution fusion | flops 19383975936 | bytes 47185920 | tf_op jit(solution)/shard_map/dot_general | solution.py:109
  (2 shorter events, 0.0 us)
Async XLA Ops:
  1.4 11.7 %collective-permute-start = (bf16[768,128]{1,0:T(8,128)(2,1)S(1)}, bf16[768,128]{1,0:T(8,128)(2,1)S(1)}, u32[]{:S(2)}, u32[]{:S(2)}) collective-permute-start(bf16[768,128]{1,0:T(8,128)(2,1)S(1)} %fusion.19), channel_id=1, source_target_pairs={{0,0},{1,8},{2,16},{3,24},{4,1},{5,9},{6,17},{7,25},{8,2},{9,10},{... | collective-permute-start | bytes 589832 | tf_op jit(solution)/shard_map/ppermute | solution.py:94
  24.8 1.0 copy-start
  67.7 10.7 %collective-permute-start.1 = (bf16[768,128]{1,0:T(8,128)(2,1)S(1)}, bf16[768,128]{1,0:T(8,128)(2,1)S(1)}, u32[]{:S(2)}, u32[]{:S(2)}) collective-permute-start(bf16[768,128]{1,0:T(8,128)(2,1)S(1)} %shard_map.28), channel_id=1, source_target_pairs={{0,0},{1,8},{2,16},{3,24},{4,1},{5,9},{6,17},{7,25},{8,2},{9,10},{... | collective-permute-start | bytes 589832 | tf_op jit(solution)/shard_map/ppermute | solution.py:94
  90.0 0.9 copy-start.1
  132.2 10.9 %collective-permute-start.2 = (bf16[768,128]{1,0:T(8,128)(2,1)S(1)}, bf16[768,128]{1,0:T(8,128)(2,1)S(1)}, u32[]{:S(2)}, u32[]{:S(2)}) collective-permute-start(bf16[768,128]{1,0:T(8,128)(2,1)S(1)} %shard_map.29), channel_id=1, source_target_pairs={{0,0},{1,8},{2,16},{3,24},{4,1},{5,9},{6,17},{7,25},{8,2},{9,10},{... | collective-permute-start | bytes 589832 | tf_op jit(solution)/shard_map/ppermute | solution.py:94
  155.1 0.9 copy-start.2
  197.4 10.9 %collective-permute-start.3 = (bf16[768,128]{1,0:T(8,128)(2,1)S(1)}, bf16[768,128]{1,0:T(8,128)(2,1)S(1)}, u32[]{:S(2)}, u32[]{:S(2)}) collective-permute-start(bf16[768,128]{1,0:T(8,128)(2,1)S(1)} %shard_map.30), channel_id=1, source_target_pairs={{0,0},{1,8},{2,16},{3,24},{4,1},{5,9},{6,17},{7,25},{8,2},{9,10},{... | collective-permute-start | bytes 589832 | tf_op jit(solution)/shard_map/ppermute | solution.py:94
